TPU v7x, 32 devices: a whole 2x2x4 slice. The times are simulated.
32 devices in a mesh: groups: 2 (over x), dp: 8 (over z, y), fsdp: 2 (over core).
Axes of the slice: x: 2, y: 2, z: 4, core: 2. Of those that a mesh axis runs over, the one named last changes fastest.
Arguments:
- hidden: bfloat16 [8192, 8192], P(('groups', 'dp', 'fsdp')), parts along dimension 0, may hold values from -600 to 600
- norm_gain: bfloat16 [8192], P('fsdp'), may hold values from 0.099609375 to 1.8984375
- w_query: bfloat16 [8192, 512], P('fsdp'), may hold values from -0.06629126 to 0.06629126
- w_key: bfloat16 [8192, 128], P('fsdp'), may hold values from -0.0625 to 0.0625
- w_value: bfloat16 [8192, 128], P('fsdp'), may hold values from -0.0625 to 0.0625
- b_query: bfloat16 [512], replicated, may hold values from -3 to 3
- b_key: bfloat16 [128], replicated, may hold values from -40 to 40
- b_value: bfloat16 [128], replicated, may hold values from -3 to 3
- row_host: int32 [8192], P(('groups', 'dp', 'fsdp')), parts along dimension 0, may hold values from 0 to 15, as said below
- row_slot: int32 [8192], P(('groups', 'dp', 'fsdp')), parts along dimension 0, may hold values from 0 to 7
Outputs:
- context: bfloat16 [8192, 512], P(('groups', 'dp', 'fsdp')), parts along dimension 0
There are 2 independent parts, one for each index of `groups`. A program takes and returns all parts, laid end to end along the dimension named above; an argument that names none is the same for every part. Nothing has to cross between parts.
Inputs may be any that keep to these rules, and one draw needn't show every extreme that they name: `row_host`: index of the hosting device along dp and fsdp together. Of one device's rows at most 32 go to one host; in every draw some host receives exactly 32 rows from every device.
All inputs are finite; a program needn't handle non-finite values.
Results may differ from a plain program's by a relative error of at most 0.012.
The roundings to bfloat16 on the way count: a program that leaves them out, or rounds other values in their place, can miss the bound.
Values may be sent and summed in bfloat16 or wider, within the bound.
No kernel may reach another device: no remote copies, remote signals or barrier semaphores. Data moves between devices by JAX's collectives and lax.ppermute only.
A program may use at most 128 MiB of HBM per device.

v0:
```python
import functools
import jax
import jax.numpy as jnp
import numpy as np
from jax import lax
from jax.experimental import pallas as pl
from jax.experimental.pallas import tpu as pltpu
from jax.sharding import PartitionSpec as P

HD = 128
HQ = 4
QW = HQ * HD
SLOTS_PER_HOST = 8
BLOCK = 32
LARGE = 1e30
FACTS = 16
KV_MIB = 56
rope_base = 1000000.0
epsilon = 1e-06
f32 = jnp.float32
bf16 = jnp.bfloat16
i32 = jnp.int32
MIB = 1024 * 1024
ANYWHERE = pl.BlockSpec(memory_space=pltpu.HBM)
FREE = pl.BlockSpec(memory_space=pl.ANY)


def params(mib=58):
    return pltpu.CompilerParams(vmem_limit_bytes=mib * MIB)


def whole(shape):
    return pl.BlockSpec(shape, lambda *i: (0,) * len(shape))


def rotary_table(positions):
    frequency = np.power(np.float32(rope_base), -np.arange(HD // 2, dtype=np.float32) * np.float32(2.0 / HD))
    rotation = np.arange(positions, dtype=np.float32)[:, None] * frequency.astype(np.float32)[None, :]
    rotation = rotation.astype(np.float64)
    rest = np.concatenate([np.cos(rotation), np.sin(rotation)], axis=1).astype(np.float32)
    terms = []
    for _ in range(2):
        term = rest.astype(jnp.bfloat16)
        terms.append(term)
        rest = rest - term.astype(np.float32)
    return np.concatenate(terms, axis=1)


def key_value_kernel(core_ref, hidden_hbm, *rest):
    weights_hbm, small_hbm, rest = rest[:4], rest[4:10], rest[10:]
    out_ref, normed_hbm, hidden, normed, gains, wk, wv, wk_other, wv_other, *rest = rest
    small, (in_sems, sems, out_sems) = rest[:6], rest[6:]
    gain_ref, gain_other_ref, bk_ref, bv_ref, host_ref, slot_ref = small
    rows, width = hidden.shape
    half = width // 2
    core = core_ref[0]
    own_at = pl.multiple_of(core * half, half)
    other_at = pl.multiple_of((1 - core) * half, half)
    parts = in_sems.shape[0]
    part_rows = rows // parts
    lanes = 1024
    high = 8

    small_copies = [pltpu.make_async_copy(a, b, sems.at[4 + i]) for i, (a, b) in enumerate(zip(small_hbm, small))]
    weights = (wk, wv, wk_other, wv_other)
    weight_copies = [pltpu.make_async_copy(a, b, sems.at[i]) for i, (a, b) in enumerate(zip(weights_hbm, weights))]

    def span(i):
        return pl.ds(i * part_rows, part_rows)

    loads = [pltpu.make_async_copy(hidden_hbm.at[span(i), :], hidden.at[span(i), :], in_sems.at[i]) for i in range(parts)]
    saves = [pltpu.make_async_copy(normed.at[span(i), :], normed_hbm.at[span(i), :], out_sems.at[i]) for i in range(parts)]
    for c in small_copies + loads + weight_copies:
        c.start()
    for c in small_copies:
        c.wait()
    gains[:, pl.ds(own_at, half)] = jnp.broadcast_to(gain_ref[...].astype(f32)[None, :], (high, half))
    gains[:, pl.ds(other_at, half)] = jnp.broadcast_to(gain_other_ref[...].astype(f32)[None, :], (high, half))
    tail = out_ref.shape[0] - rows
    line = lax.broadcasted_iota(i32, (tail, rows), 0)
    facts = jnp.where(line == 0, host_ref[...][None, :], jnp.where(line == 1, slot_ref[...][None, :], 0))
    out_ref[rows:, :] = facts.astype(f32).astype(bf16)

    for i in range(parts):
        at = slice(i * part_rows, (i + 1) * part_rows)
        loads[i].wait()
        total = jnp.zeros((part_rows, lanes), f32)
        for j in range(width // lanes):
            wide = hidden[at, j * lanes : (j + 1) * lanes].astype(f32)
            total += wide * wide
        mean = jnp.sum(total, axis=1, keepdims=True) * (1.0 / width)
        scale = lax.rsqrt(mean + epsilon)
        for j in range(width // lanes):
            to = slice(j * lanes, (j + 1) * lanes)
            wide = (hidden[at, to].astype(f32) * scale).reshape(part_rows // high, high, lanes)
            normed[at, to] = (wide * gains[:, to][None]).reshape(part_rows, lanes).astype(bf16)
        saves[i].start()
    for c in weight_copies[:2]:
        c.wait()
    total = jnp.dot(
        normed[:, pl.ds(own_at, half)], jnp.concatenate([wk[...], wv[...]], axis=1), preferred_element_type=f32
    )
    for c in weight_copies[2:]:
        c.wait()
    total += jnp.dot(
        normed[:, pl.ds(other_at, half)],
        jnp.concatenate([wk_other[...], wv_other[...]], axis=1),
        preferred_element_type=f32,
    )
    out_ref[:rows, :HD] = (total[:, :HD] + bk_ref[...].astype(f32)[None, :]).astype(bf16)
    out_ref[:rows, HD:] = (total[:, HD:] + bv_ref[...].astype(f32)[None, :]).astype(bf16)
    for c in saves:
        c.wait()


def keys_and_values(core, hidden, w_key, w_value, wk_other, wv_other, *small):
    rows, width = hidden.shape
    half = width // 2
    parts = 8
    vmem = pl.BlockSpec(memory_space=pltpu.VMEM)
    return pl.pallas_call(
        key_value_kernel,
        in_specs=[pl.BlockSpec(memory_space=pltpu.SMEM)] + [ANYWHERE] * 3 + [FREE] * (2 + len(small)),
        out_specs=[vmem, ANYWHERE],
        out_shape=[
            jax.ShapeDtypeStruct((rows + FACTS, 2 * HD), bf16),
            jax.ShapeDtypeStruct((rows, width), bf16),
        ],
        scratch_shapes=[
            pltpu.VMEM((rows, width), bf16),
            pltpu.VMEM((rows, width), bf16),
            pltpu.VMEM((8, width), f32),
            *[pltpu.VMEM((half, HD), bf16)] * 4,
            *[pltpu.VMEM(a.shape, a.dtype) for a in small],
            pltpu.SemaphoreType.DMA((parts,)),
            pltpu.SemaphoreType.DMA((4 + len(small),)),
            pltpu.SemaphoreType.DMA((parts,)),
        ],
        compiler_params=params(62),
        cost_estimate=pl.CostEstimate(flops=8 * rows * half * HD, bytes_accessed=10 * MIB, transcendentals=0),
        name="keys_values",
    )(core, hidden, w_key, w_value, wk_other, wv_other, *small)


def query_kernel(mine, core_ref, rows_hbm, weights_hbm, *rest):
    if mine:
        out_ref, rows, weights, sems = rest
    else:
        sum_hbm, b_hbm, out_ref, rows, weights, total_ref, b_ref, sems = rest
    half = weights.shape[0]
    parts = 4
    chunk = half // parts
    side = core_ref[0] if mine else 1 - core_ref[0]
    copies = []
    for i in range(parts):
        at = pl.ds(i * chunk, chunk)
        source = pl.ds(pl.multiple_of(side * half + i * chunk, chunk), chunk)
        copies.append(pltpu.make_async_copy(rows_hbm.at[:, source], rows.at[:, at], sems.at[2 * i]))
        copies.append(pltpu.make_async_copy(weights_hbm.at[at, :], weights.at[at, :], sems.at[2 * i + 1]))
    if not mine:
        copies.append(pltpu.make_async_copy(sum_hbm, total_ref, sems.at[2 * parts]))
        copies.append(pltpu.make_async_copy(b_hbm, b_ref, sems.at[2 * parts + 1]))
    for c in copies:
        c.start()
    total = None
    for i in range(parts):
        copies[2 * i].wait()
        copies[2 * i + 1].wait()
        at = slice(i * chunk, (i + 1) * chunk)
        here = jnp.dot(rows[:, at], weights[at, :], preferred_element_type=f32)
        total = here if total is None else total + here
    if mine:
        out_ref[...] = total
    else:
        copies[-2].wait()
        copies[-1].wait()
        out_ref[...] = (total + total_ref[...] + b_ref[...].astype(f32)[None, :]).astype(bf16)


def query_half(mine, core, normed, weights, *more):
    rows = normed.shape[0]
    half = weights.shape[0]
    extra = [] if mine else [pltpu.VMEM((rows, QW), f32), pltpu.VMEM((QW,), bf16)]
    return pl.pallas_call(
        functools.partial(query_kernel, mine),
        in_specs=[pl.BlockSpec(memory_space=pltpu.SMEM)] + [ANYWHERE] * (2 + len(more)),
        out_shape=jax.ShapeDtypeStruct((rows, QW), f32 if mine else bf16),
        scratch_shapes=[
            pltpu.VMEM((rows, half), bf16),
            pltpu.VMEM((half, QW), bf16),
            *extra,
            pltpu.SemaphoreType.DMA((10,)),
        ],
        compiler_params=params(KV_MIB),
        cost_estimate=pl.CostEstimate(flops=2 * rows * half * QW, bytes_accessed=6 * MIB, transcendentals=0),
        name="queries_own" if mine else "queries_other",
    )(core, normed, weights, *more)


class Group:
    def __init__(self, pieces, rows, capacity, seq_count, lower_ref, usable_ref, before_count, first):
        self.pieces = pieces
        count = len(pieces)
        shift = SLOTS_PER_HOST.bit_length() - 1
        facts = [p[rows:, :].astype(f32) for p in pieces]
        hosts = jnp.concatenate([f[0:1] for f in facts], axis=0).astype(i32)
        seqs = hosts * SLOTS_PER_HOST + jnp.concatenate([f[1:2] for f in facts], axis=0).astype(i32)
        padded = jnp.concatenate([seqs, jnp.zeros((HD - count, rows), i32)], axis=0)
        columns = jnp.transpose(padded.astype(f32)).astype(i32)
        at_row = lax.broadcasted_iota(i32, (rows, rows), 0)
        at_lane = lax.broadcasted_iota(i32, (rows, rows), 1)
        before = jnp.where(at_row < at_lane, 1, 0)
        below = jnp.where(at_lane < at_row, 1.0, 0.0).astype(bf16)
        seq_lanes = lax.broadcasted_iota(i32, (rows, seq_count), 1)
        code_lanes = lax.broadcasted_iota(i32, (rows, HD), 1)
        codes_in_block = SLOTS_PER_HOST * BLOCK // capacity
        hots, counts, self.slots, self.marks = [], [], [], []
        for p in range(count):
            column = columns[:, p : p + 1]
            hot = jnp.where(seq_lanes == column, 1.0, 0.0)
            hots.append(hot)
            counts.append(jnp.sum(hot, axis=0, keepdims=True))
            same = lax.shift_right_logical(column, shift) == hosts[p : p + 1, :]
            rank = jnp.sum(jnp.where(same, before, 0), axis=0, keepdims=True)
            self.slots.append(hosts[p : p + 1, :] * capacity + rank)
            code = jnp.where(usable_ref[first + p] > 0, lax.bitwise_and(column, codes_in_block - 1), -1)
            mark = (code_lanes == code) | ((code_lanes == HD - 1) & (code >= 0))
            self.marks.append(jnp.where(mark, 1.0, 0.0).astype(bf16))
        base = jnp.zeros((count, seq_count), f32) + before_count
        for q in range(count):
            base = base + lower_ref[first : first + count, first + q : first + q + 1] * counts[q]
        self.positions = []
        ranks = jnp.dot(below, jnp.concatenate(hots, axis=1).astype(bf16), preferred_element_type=f32)
        for p in range(count):
            earlier = ranks[:, p * seq_count : (p + 1) * seq_count] + base[p : p + 1, :]
            self.positions.append(jnp.sum(hots[p] * earlier, axis=1, keepdims=True).astype(i32))
        self.count = before_count
        for q in range(count):
            self.count = self.count + jnp.where(usable_ref[first + q] > 0, counts[q], 0.0)

    def turns(self, table):
        position = jnp.concatenate(self.positions, axis=0)
        places = lax.broadcasted_iota(i32, (position.shape[0], table.shape[0]), 1)
        hot = jnp.where(places == position, 1.0, 0.0).astype(bf16)
        terms = jnp.dot(hot, table[...], preferred_element_type=f32)
        return terms[:, :HD] + terms[:, HD:]


def turned(block, turn):
    half = HD // 2
    first = lax.broadcasted_iota(i32, block.shape, 1) < half
    other_turn = pltpu.roll(turn, half, 1)
    cosine = jnp.where(first, turn, other_turn)
    sine = jnp.where(first, -other_turn, turn)
    return block * cosine + pltpu.roll(block, half, 1) * sine


def one_hot(slot_row, slots):
    rows = slot_row.shape[1]
    at = lax.broadcasted_iota(i32, (slots, rows), 0)
    return jnp.where(at == slot_row, 1.0, 0.0).astype(bf16)


def spread_group(group, rows, table, keys, values, at_piece):
    blocks = keys.shape[0]
    slots = blocks * BLOCK
    last = lax.broadcasted_iota(i32, (slots, HD), 1) == HD - 1
    turns = group.turns(table)
    raw = jnp.concatenate([piece[:rows, :HD] for piece in group.pieces], axis=0)
    own_keys = turned(raw.astype(f32), turns).astype(bf16)
    for p, piece in enumerate(group.pieces):
        hot = one_hot(group.slots[p], slots)
        at = slice((at_piece + p) * BLOCK, (at_piece + p + 1) * BLOCK)
        both = jnp.concatenate([own_keys[p * rows : (p + 1) * rows], group.marks[p], piece[:rows, HD:]], axis=1)
        moved = jnp.dot(hot, both, preferred_element_type=f32)
        marks = moved[:, HD : 2 * HD]
        marks = jnp.where(last, 1.0 - marks, marks)
        keys[:, at, :HD] = moved[:, :HD].astype(bf16).reshape(blocks, BLOCK, HD)
        keys[:, at, HD:] = marks.astype(bf16).reshape(blocks, BLOCK, HD)
        values[:, at, :] = moved[:, 2 * HD :].astype(bf16).reshape(blocks, BLOCK, HD)
    return turns


def early_kernel(count, capacity, seq_count, first, usable_ref, table, lower_ref, *rest):
    piece_refs = rest[:count]
    keys, values, count_ref = rest[count:]
    rows = piece_refs[0].shape[0] - FACTS
    group = Group(piece_refs, rows, capacity, seq_count, lower_ref, usable_ref, 0.0, first)
    spread_group(group, rows, table, keys, values, 0)
    count_ref[...] = group.count


def spread_early(usable, table, lower, pieces, first, capacity, seq_count, slots):
    vmem = pl.BlockSpec(memory_space=pltpu.VMEM)
    blocks = slots // BLOCK
    length = len(pieces) * BLOCK
    return pl.pallas_call(
        functools.partial(early_kernel, len(pieces), capacity, seq_count, first),
        in_specs=[pl.BlockSpec(memory_space=pltpu.SMEM)] + [vmem] * (2 + len(pieces)),
        out_shape=[
            jax.ShapeDtypeStruct((blocks, length, 2 * HD), bf16),
            jax.ShapeDtypeStruct((blocks, length, HD), bf16),
            jax.ShapeDtypeStruct((1, seq_count), f32),
        ],
        compiler_params=params(16),
        name="spread_early",
    )(usable, table, lower, *pieces)


def attention_kernel(count, capacity, seq_count, usable_ref, table, lower_ref, q_hbm, *rest):
    early_keys, early_values, early_count, *rest = rest
    before_count = early_count[...]
    piece_refs = rest[:count]
    out_ref, keys, values, contexts, scores_ref, weights_ref, q_ref, q_sem = rest[count:]
    load = pltpu.make_async_copy(q_hbm, q_ref, q_sem)
    load.start()
    blocks = keys.shape[0]
    slots = blocks * BLOCK
    rows = q_ref.shape[0]
    group = Group(piece_refs, rows, capacity, seq_count, lower_ref, usable_ref, before_count, 0)
    own_turn = spread_group(group, rows, table, keys, values, 0)[:rows]
    load.wait()
    queries = [turned(q_ref[:, h * HD : (h + 1) * HD].astype(f32), own_turn).astype(bf16) for h in range(HQ)]
    own_hot = one_hot(group.slots[0], slots)
    last = lax.broadcasted_iota(i32, (slots, HD), 1) == HD - 1
    q_slots = jnp.dot(own_hot, jnp.concatenate(queries, axis=1), preferred_element_type=f32).astype(bf16)
    q_marks = jnp.dot(own_hot, group.marks[0], preferred_element_type=f32)
    q_marks = (jnp.where(last, -1.0, q_marks - 1.0) * LARGE).astype(bf16)
    late = keys.shape[1]
    height = HQ * BLOCK
    contract = (((1,), (1,)), ((), ()))
    for block in range(blocks):
        at = slice(block * BLOCK, (block + 1) * BLOCK)
        q_block = q_slots[at, :]
        marks = q_marks[at, :]
        q_heads = jnp.concatenate(
            [jnp.concatenate([q_block[:, h * HD : (h + 1) * HD], marks], axis=1) for h in range(HQ)], axis=0
        )
        to = slice(block * height, (block + 1) * height)
        scores_ref[to, :late] = lax.dot_general(q_heads, keys[block], contract, preferred_element_type=f32)
        scores_ref[to, late:] = lax.dot_general(q_heads, early_keys[block], contract, preferred_element_type=f32)
    q_index = lax.broadcasted_iota(i32, (height, HD), 0) % BLOCK
    k_index = lax.broadcasted_iota(i32, (height, HD), 1)
    ordered = (k_index >= BLOCK) | (k_index <= q_index)
    rate = HD ** (-0.5)
    for block in range(blocks):
        to = slice(block * height, (block + 1) * height)
        scores = scores_ref[to, :]
        scores = jnp.concatenate([jnp.where(ordered, scores[:, :HD], -LARGE), scores[:, HD:]], axis=1)
        exponent = jnp.exp((scores - jnp.max(scores, axis=1, keepdims=True)) * rate)
        weights_ref[to, :] = (exponent * (1.0 / jnp.sum(exponent, axis=1, keepdims=True))).astype(bf16)
    for block in range(blocks):
        at = slice(block * BLOCK, (block + 1) * BLOCK)
        to = slice(block * height, (block + 1) * height)
        context = jnp.dot(weights_ref[to, :late], values[block], preferred_element_type=f32)
        context += jnp.dot(weights_ref[to, late:], early_values[block], preferred_element_type=f32)
        context = context.astype(bf16)
        for h in range(HQ):
            contexts[at, h * HD : (h + 1) * HD] = context[h * BLOCK : (h + 1) * BLOCK, :]
    out_ref[...] = lax.dot_general(
        own_hot, contexts[...], (((0,), (0,)), ((), ())), preferred_element_type=f32
    ).astype(bf16)


def attend(usable, table, lower, queries, early, pieces, capacity, seq_count, slots):
    rows = queries.shape[0]
    blocks = slots // BLOCK
    vmem = pl.BlockSpec(memory_space=pltpu.VMEM)
    count = len(pieces)
    late = count * BLOCK
    total = late + early[0].shape[1]
    height = blocks * HQ * BLOCK
    return pl.pallas_call(
        functools.partial(attention_kernel, count, capacity, seq_count),
        in_specs=[pl.BlockSpec(memory_space=pltpu.SMEM), vmem, vmem, FREE] + [vmem] * (len(early) + count),
        out_shape=jax.ShapeDtypeStruct((rows, QW), bf16),
        scratch_shapes=[
            pltpu.VMEM((blocks, late, 2 * HD), bf16),
            pltpu.VMEM((blocks, late, HD), bf16),
            pltpu.VMEM((slots, QW), bf16),
            pltpu.VMEM((height, total), f32),
            pltpu.VMEM((height, total), bf16),
            pltpu.VMEM((rows, QW), bf16),
            pltpu.SemaphoreType.DMA,
        ],
        compiler_params=params(24),
        name="attention",
    )(usable, table, lower, queries, *early, *pieces)


def rotary(tensor, position):
    half_dim = tensor.shape[-1] // 2
    frequency = jnp.power(
        rope_base, -jnp.arange(half_dim, dtype=jnp.float32) * 2.0 / tensor.shape[-1]
    )
    rotation = position.astype(jnp.float32)[:, None] * frequency[None, :]
    cosine = jnp.cos(rotation)[:, None, :]
    sine_part = jnp.sin(rotation)[:, None, :]
    front_half = tensor[..., :half_dim]
    back_half = tensor[..., half_dim:]
    return jnp.concatenate(
        [front_half * cosine - back_half * sine_part, back_half * cosine + front_half * sine_part],
        axis=-1,
    )


def finish(query_sum, key_sum, value_sum, b_query, b_key, b_value):
    return jnp.concatenate(
        [
            (query_sum + b_query.astype(jnp.float32)).astype(jnp.bfloat16),
            (key_sum + b_key.astype(jnp.float32)).astype(jnp.bfloat16),
            (value_sum + b_value.astype(jnp.float32)).astype(jnp.bfloat16),
        ],
        axis=1,
    )


def project(source_rows, norm_gain, w_query, w_key, w_value, b_query, b_key, b_value):
    widened = source_rows.astype(jnp.float32)
    inverse = lax.rsqrt(jnp.mean(widened * widened, axis=1, keepdims=True) + epsilon)
    query_part = lax.all_gather(w_query, "fsdp", axis=0, tiled=True)
    key_part = lax.all_gather(w_key, "fsdp", axis=0, tiled=True)
    value_part = lax.all_gather(w_value, "fsdp", axis=0, tiled=True)
    gain_part = lax.all_gather(norm_gain, "fsdp", axis=0, tiled=True)
    normed_part = (
        source_rows.astype(jnp.float32) * inverse * gain_part.astype(jnp.float32)
    ).astype(jnp.bfloat16)
    query_sum = jnp.dot(normed_part, query_part, preferred_element_type=jnp.float32)
    key_sum = jnp.dot(normed_part, key_part, preferred_element_type=jnp.float32)
    value_sum = jnp.dot(normed_part, value_part, preferred_element_type=jnp.float32)
    return finish(query_sum, key_sum, value_sum, b_query, b_key, b_value)


def attend_at_host(projected, slot_ids):
    row_count = projected.shape[0]
    query_width = HQ * HD
    queries = projected[:, :query_width].reshape(row_count, HQ, HD)
    keys_raw = projected[:, query_width : query_width + HD]
    values_raw = projected[:, query_width + HD :]
    index_row = jnp.arange(row_count)
    same_slot = slot_ids[:, None] == slot_ids[None, :]
    position = jnp.sum(same_slot & (index_row[None, :] < index_row[:, None]), axis=1)
    allowed = same_slot & (index_row[None, :] <= index_row[:, None])
    query_rot = rotary(queries.astype(jnp.float32), position).astype(jnp.bfloat16)
    key_rot = rotary(keys_raw.astype(jnp.float32)[:, None, :], position)[:, 0, :].astype(
        jnp.bfloat16
    )
    scores = jnp.einsum(
        "qhd,kd->hqk", query_rot, key_rot, preferred_element_type=jnp.float32
    ) * HD ** (-0.5)
    scores = jnp.where(allowed[None, :, :], scores, -jnp.inf)
    largest = jnp.max(scores, axis=-1, keepdims=True)
    exponent = jnp.exp(scores - largest)
    attention = (exponent / jnp.sum(exponent, axis=-1, keepdims=True)).astype(jnp.bfloat16)
    context = jnp.einsum("hqk,kd->qhd", attention, values_raw, preferred_element_type=jnp.float32)
    return context.astype(jnp.bfloat16).reshape(row_count, query_width)


def per_device_exchanged(
    hidden, norm_gain, w_query, w_key, w_value, b_query, b_key, b_value, row_host, row_slot
):
    host_count = lax.axis_size(("dp", "fsdp"))
    source_count = hidden.shape[0]
    capacity = 2 * source_count // host_count
    index_row = jnp.arange(source_count)
    same_host = row_host[:, None] == row_host[None, :]
    row_rank = jnp.sum(same_host & (index_row[None, :] < index_row[:, None]), axis=1)
    slot_index = row_host * capacity + row_rank
    payload = project(hidden, norm_gain, w_query, w_key, w_value, b_query, b_key, b_value)
    payload_width = payload.shape[1]
    outgoing = (
        jnp.zeros((host_count * capacity, payload_width), jnp.bfloat16).at[slot_index].set(payload)
    )
    slot_out = jnp.full((host_count * capacity,), -1, jnp.int32).at[slot_index].set(row_slot)
    arrived, slot_ids = (
        lax.all_to_all(
            outgoing.reshape(host_count, capacity, payload_width),
            ("dp", "fsdp"),
            split_axis=0,
            concat_axis=0,
            tiled=True,
        ),
        lax.all_to_all(
            slot_out.reshape(host_count, capacity),
            ("dp", "fsdp"),
            split_axis=0,
            concat_axis=0,
            tiled=True,
        ),
    )
    arrived = arrived.reshape(host_count * capacity, payload_width)
    slot_ids = slot_ids.reshape(host_count * capacity)
    context = attend_at_host(arrived, slot_ids)
    returned = lax.all_to_all(
        context.reshape(host_count, capacity, context.shape[1]),
        ("dp", "fsdp"),
        split_axis=0,
        concat_axis=0,
        tiled=True,
    )
    return returned.reshape(host_count * capacity, context.shape[1])[slot_index]


def swap_cores(array):
    return lax.ppermute(array, "fsdp", [(0, 1), (1, 0)])


def far(array, shift):
    count = lax.axis_size("dp")
    return lax.ppermute(array, "dp", [(i, (i + shift * 2) % count) for i in range(count)])


def swap_near(array):
    count = lax.axis_size("dp")
    return lax.ppermute(array, "dp", [(i, i ^ 1) for i in range(count)])


def after(array, *others):
    return lax.optimization_barrier((array, *others))[0]


def per_device_stepped(
    hidden, norm_gain, w_query, w_key, w_value, b_query, b_key, b_value, row_host, row_slot
):
    host_count = lax.axis_size(("dp", "fsdp"))
    rows = hidden.shape[0]
    capacity = 2 * rows // host_count
    slots = host_count * capacity
    seq_count = host_count * SLOTS_PER_HOST
    row, core = lax.axis_index("dp"), lax.axis_index("fsdp")
    me = lax.axis_index(("dp", "fsdp"))
    index = jnp.arange(host_count)
    far_row = (row // 2 - index // 4) % 4
    sources = far_row * 4 + ((row % 2) ^ ((index // 2) % 2)) * 2 + (core ^ (index % 2))
    usable = (sources <= me).astype(i32)
    lower = ((sources[None, :] < sources[:, None]) & (usable[None, :] > 0)).astype(f32)
    table = jnp.asarray(rotary_table(2 * rows))
    which = core.reshape(1)

    gain_other = swap_cores(norm_gain)
    w_value_other = swap_cores(w_value)
    w_key_other = swap_cores(w_key)
    pairs, normed = keys_and_values(
        which, hidden, w_key, w_value, w_key_other, w_value_other,
        norm_gain, gain_other, b_key, b_value, row_host, row_slot,
    )
    w_query_other = swap_cores(after(w_query, w_key_other, w_value_other, gain_other))
    first_half = query_half(True, which, normed, w_query)
    lines = {0: pairs}
    for shift in (2, 3, 1):
        lines[shift] = far(pairs, shift)
    queries = query_half(False, which, normed, w_query_other, first_half, b_query)
    nears = [swap_near(after(lines[shift], queries) if shift in (1, 2) else lines[shift]) for shift in range(4)]
    early_pieces = []
    for shift in (2, 3):
        for here in (lines[shift], nears[shift]):
            early_pieces += [here, swap_cores(here)]
    early = spread_early(usable, table, lower, early_pieces, 8, capacity, seq_count, slots)
    late = []
    for shift in (0, 1):
        for here in (lines[shift], nears[shift]):
            sent = after(here, early[2]) if shift == 1 and here is nears[1] else here
            late += [here, swap_cores(sent)]
    return attend(usable, table, lower, queries, early, late, capacity, seq_count, slots)


def per_device(*args):
    if lax.axis_size("dp") == 8:
        return per_device_stepped(*args)
    return per_device_exchanged(*args)


def solution(mesh):
    return jax.shard_map(
        per_device,
        mesh=mesh,
        in_specs=(
            P(("groups", "dp", "fsdp"), None),
            P("fsdp"),
            P("fsdp", None),
            P("fsdp", None),
            P("fsdp", None),
            P(),
            P(),
            P(),
            P(("groups", "dp", "fsdp")),
            P(("groups", "dp", "fsdp")),
        ),
        out_specs=P(("groups", "dp", "fsdp"), None),
        check_vma=False,
    )
```

profile of v0, /device:TPU:0, one launch (start us, length us, event | category | flops | bytes accessed | tf_op | source)
XLA Modules:
  0.0 53.2 jit_solution(9476598934859309783)
XLA Ops:
  0.0 0.5 collective-permute-start
  0.5 0.1 collective-permute-start.1
  0.5 0.5 collective-permute-start.2
  1.0 2.9 %collective-permute-done.2.rest_5_ = bf16[4096]{0:T(1024)(128)(2,1)S(1)} collective-permute-done((bf16[4096]{0:T(1024)(128)(2,1)}, bf16[4096]{0:T(1024)(128)(2,1)S(1)}, u32[]{:S(2)}, u32[]{:S(2)}) %collective-permute-start.2) | collective-permute-done | bytes 8224 | tf_op jit(solution)/shard_map/ppermute | solution.py:505
  3.9 0.7 %collective-permute-done.1.rest_3_ = bf16[4096,128]{1,0:T(8,128)(2,1)} collective-permute-done((bf16[4096,128]{1,0:T(8,128)(2,1)}, bf16[4096,128]{1,0:T(8,128)(2,1)}, u32[]{:S(2)}, u32[]{:S(2)}) %collective-permute-start.1) | collective-permute-done | bytes 1048608 | tf_op jit(solution)/shard_map/ppermute | solution.py:505
  4.6 0.4 collective-permute-start.3
  5.0 0.0 copy-done.3
  5.0 6.9 %keys_values.1 = (bf16[272,256]{1,0:T(8,128)(2,1)}, bf16[256,8192]{1,0:T(8,128)(2,1)}) custom-call(s32[1]{0:T(128)} %bitcast.core_ref, bf16[256,8192]{1,0:T(8,128)(2,1)} %hidden_hbm.1, bf16[4096,128]{1,0:T(8,128)(2,1)} %rest_0_.1, bf16[4096,128]{1,0:T(8,128)(2,1)} %rest_1_.2, bf16[4096,128]{1,0:T(8,128)(2,1)} %copy-done.3, ...), custom_call_target="tpu_custom_call" | custom-call | flops 1073741824 | bytes 10485760 | tf_op jit(solution)/shard_map/keys_values/pallas_call | solution.py:121
  11.9 5.6 %collective-permute-start.8 = (bf16[272,256]{1,0:T(8,128)(2,1)}, bf16[272,256]{1,0:T(8,128)(2,1)S(1)}, u32[]{:S(2)}, u32[]{:S(2)}) collective-permute-start(bf16[272,256]{1,0:T(8,128)(2,1)} %get-tuple-element.16.rest_3_), channel_id=1, source_target_pairs={{0,12},{2,14},{4,0},{6,2},{8,4},{10,6},{12,8},{14,10},{1,13},{3,15... | collective-permute-start | bytes 417800 | tf_op jit(solution)/shard_map/ppermute | solution.py:510
  17.5 1.0 %collective-permute-start.15 = (bf16[272,256]{1,0:T(8,128)(2,1)}, bf16[272,256]{1,0:T(8,128)(2,1)S(1)}, u32[]{:S(2)}, u32[]{:S(2)}) collective-permute-start(bf16[272,256]{1,0:T(8,128)(2,1)} %get-tuple-element.16.rest_3_), channel_id=1, source_target_pairs={{0,4},{2,6},{4,8},{6,10},{8,12},{10,14},{12,0},{14,2},{1,5},{3,7},... | collective-permute-start | bytes 417800 | tf_op jit(solution)/shard_map/ppermute | solution.py:510
  18.5 1.5 %collective-permute-start.13 = (bf16[272,256]{1,0:T(8,128)(2,1)}, bf16[272,256]{1,0:T(8,128)(2,1)S(1)}, u32[]{:S(2)}, u32[]{:S(2)}) collective-permute-start(bf16[272,256]{1,0:T(8,128)(2,1)} %get-tuple-element.16.rest_3_), channel_id=1, source_target_pairs={{0,2},{2,0},{4,6},{6,4},{8,10},{10,8},{12,14},{14,12},{1,3},{3,1},... | collective-permute-start | bytes 417800 | tf_op jit(solution)/shard_map/ppermute | solution.py:515
  20.0 4.2 %queries_own.1.rest_0_ = f32[256,512]{1,0:T(8,128)} custom-call(s32[1]{0:T(128)} %bitcast.core_ref, bf16[256,8192]{1,0:T(8,128)(2,1)} %get-tuple-element.14.rows_hbm, bf16[4096,512]{1,0:T(8,128)(2,1)} %weights_hbm.1), custom_call_target="tpu_custom_call" | custom-call | flops 1073741824 | bytes 6291456 | tf_op jit(solution)/shard_map/queries_own/pallas_call | solution.py:184
  24.2 0.0 copy-start
  24.3 0.6 %collective-permute-start.10 = (bf16[272,256]{1,0:T(8,128)(2,1)S(1)}, bf16[272,256]{1,0:T(8,128)(2,1)S(1)}, u32[]{:S(2)}, u32[]{:S(2)}) collective-permute-start(bf16[272,256]{1,0:T(8,128)(2,1)S(1)} %collective-permute-done.8.rest_4_), channel_id=1, source_target_pairs={{0,2},{2,0},{4,6},{6,4},{8,10},{10,8},{12,14},{14,12},{1,3},{3,1},... | collective-permute-start | bytes 417800 | tf_op jit(solution)/shard_map/ppermute | solution.py:515
  24.8 4.1 %queries_other.1.q_hbm = bf16[256,512]{1,0:T(8,128)(2,1)} custom-call(s32[1]{0:T(128)} %bitcast.core_ref, bf16[256,8192]{1,0:T(8,128)(2,1)} %get-tuple-element.14.rows_hbm, bf16[4096,512]{1,0:T(8,128)(2,1)} %collective-permute-done.3.weights_hbm, f32[256,512]{1,0:T(8,128)} %queries_own.1.rest_0_, bf16[512]{0:T(512)(128)(2,1)} %rest_1_.3), custom_call_target="tpu_custom_call" | custom-call | flops 1073741824 | bytes 6291456 | tf_op jit(solution)/shard_map/queries_other/pallas_call | solution.py:184
  28.9 1.0 %collective-permute-done.4.rest_0_ = bf16[272,256]{1,0:T(8,128)(2,1)S(1)} collective-permute-done((bf16[272,256]{1,0:T(8,128)(2,1)}, bf16[272,256]{1,0:T(8,128)(2,1)S(1)}, u32[]{:S(2)}, u32[]{:S(2)}) %collective-permute-start.4) | collective-permute-done | bytes 139296 | tf_op jit(solution)/shard_map/ppermute | solution.py:510
  30.0 1.5 %collective-permute-start.6 = (bf16[272,256]{1,0:T(8,128)(2,1)S(1)}, bf16[272,256]{1,0:T(8,128)(2,1)S(1)}, u32[]{:S(2)}, u32[]{:S(2)}) collective-permute-start(bf16[272,256]{1,0:T(8,128)(2,1)S(1)} %collective-permute-done.4.rest_0_), channel_id=1, source_target_pairs={{0,2},{2,0},{4,6},{6,4},{8,10},{10,8},{12,14},{14,12},{1,3},{3,1},... | collective-permute-start | bytes 417800 | tf_op jit(solution)/shard_map/ppermute | solution.py:515
  31.5 0.1 collective-permute-start.5
  31.6 0.5 collective-permute-start.9
  32.1 0.1 collective-permute-start.11
  32.2 0.5 collective-permute-start.17
  32.7 2.4 %collective-permute-done.6.rest_2_ = bf16[272,256]{1,0:T(8,128)(2,1)S(1)} collective-permute-done((bf16[272,256]{1,0:T(8,128)(2,1)S(1)}, bf16[272,256]{1,0:T(8,128)(2,1)S(1)}, u32[]{:S(2)}, u32[]{:S(2)}) %collective-permute-start.6) | collective-permute-done | bytes 139296 | tf_op jit(solution)/shard_map/ppermute | solution.py:515
  35.1 0.1 and_convert_fusion.lower_ref
  35.2 0.6 %collective-permute-start.12 = (bf16[272,256]{1,0:T(8,128)(2,1)S(1)}, bf16[272,256]{1,0:T(8,128)(2,1)S(1)}, u32[]{:S(2)}, u32[]{:S(2)}) collective-permute-start(bf16[272,256]{1,0:T(8,128)(2,1)S(1)} %copy-done.2), channel_id=1, source_target_pairs={{0,1},{1,0},{2,3},{3,2},{4,5},{5,4},{6,7},{7,6},{8,9},{9,8},{10,11... | collective-permute-start | bytes 417800 | tf_op jit(solution)/shard_map/ppermute | solution.py:505
  35.8 0.1 collective-permute-start.16
  35.9 0.4 collective-permute-start.14
  36.3 0.2 collective-permute-done.7.rest_3_
  36.5 5.2 %spread_early.1 = (bf16[16,256,256]{2,1,0:T(8,128)(2,1)S(1)}, bf16[16,256,128]{2,1,0:T(8,128)(2,1)S(1)}, f32[1,128]{1,0:T(1,128)S(1)}) custom-call(s32[16]{0:T(128)S(1)} %get-tuple-element.24.usable_ref, bf16[512,256]{1,0:T(8,128)(2,1)S(1)} %copy-done, f32[16,16]{1,0:T(8,128)S(1)} %and_convert_fusion.lower_ref, ...), custom_call_target="tpu_custom_call" | custom-call | tf_op jit(solution)/shard_map/spread_early/pallas_call | solution.py:297
  41.7 0.2 collective-permute-start.18
  41.9 1.2 %collective-permute-done.18.rest_10_ = bf16[272,256]{1,0:T(8,128)(2,1)S(1)} collective-permute-done((bf16[272,256]{1,0:T(8,128)(2,1)S(1)}, bf16[272,256]{1,0:T(8,128)(2,1)S(1)}, u32[]{:S(2)}, u32[]{:S(2)}) %collective-permute-start.18) | collective-permute-done | bytes 139296 | tf_op jit(solution)/shard_map/ppermute | solution.py:505
  43.1 0.9 %copy-done.1 = bf16[256,512]{1,0:T(8,128)(2,1)S(1)} copy-done((bf16[256,512]{1,0:T(8,128)(2,1)S(1)}, bf16[256,512]{1,0:T(8,128)(2,1)}, u32[]{:S(2)}) %copy-start.1) | copy-done | bytes 262168
  44.1 9.0 %attention.1 = bf16[256,512]{1,0:T(8,128)(2,1)} custom-call(s32[16]{0:T(128)S(1)} %get-tuple-element.24.usable_ref, bf16[512,256]{1,0:T(8,128)(2,1)S(1)} %copy-done, f32[16,16]{1,0:T(8,128)S(1)} %and_convert_fusion.lower_ref, bf16[256,512]{1,0:T(8,128)(2,1)S(1)} %copy-done.1, bf16[16,256,256]{2,1,0:T(8,128)(2,1)S(1)} %get-tuple-element.18.rest_0_, ...), custom_call_target="tpu_custom_call" | custom-call | tf_op jit(solution)/shard_map/attention/pallas_call | solution.py:373
  (23 shorter events, 0.1 us)
Async XLA Ops:
  0.0 3.9 %collective-permute-start = (bf16[4096,128]{1,0:T(8,128)(2,1)}, bf16[4096,128]{1,0:T(8,128)(2,1)S(1)}, u32[]{:S(2)}, u32[]{:S(2)}) collective-permute-start(bf16[4096,128]{1,0:T(8,128)(2,1)} %rest_0_.1), channel_id=1, source_target_pairs={{0,1},{1,0},{2,3},{3,2},{4,5},{5,4},{6,7},{7,6},{8,9},{9,8},{10,11... | collective-permute-start | bytes 3145736 | tf_op jit(solution)/shard_map/ppermute | solution.py:505
  0.5 4.1 %collective-permute-start.1 = (bf16[4096,128]{1,0:T(8,128)(2,1)}, bf16[4096,128]{1,0:T(8,128)(2,1)}, u32[]{:S(2)}, u32[]{:S(2)}) collective-permute-start(bf16[4096,128]{1,0:T(8,128)(2,1)} %rest_1_.2), channel_id=1, source_target_pairs={{0,1},{1,0},{2,3},{3,2},{4,5},{5,4},{6,7},{7,6},{8,9},{9,8},{10,11... | collective-permute-start | bytes 3145736 | tf_op jit(solution)/shard_map/ppermute | solution.py:505
  0.5 3.4 %collective-permute-start.2 = (bf16[4096]{0:T(1024)(128)(2,1)}, bf16[4096]{0:T(1024)(128)(2,1)S(1)}, u32[]{:S(2)}, u32[]{:S(2)}) collective-permute-start(bf16[4096]{0:T(1024)(128)(2,1)} %rest_4_.1), channel_id=1, source_target_pairs={{0,1},{1,0},{2,3},{3,2},{4,5},{5,4},{6,7},{7,6},{8,9},{9,8},{10,11... | collective-permute-start | bytes 24584 | tf_op jit(solution)/shard_map/ppermute | solution.py:505
  3.9 1.1 %copy-start.4 = (bf16[4096]{0:T(1024)(128)(2,1)}, bf16[4096]{0:T(1024)(128)(2,1)S(1)}, u32[]{:S(2)}) copy-start(bf16[4096]{0:T(1024)(128)(2,1)S(1)} %collective-permute-done.2.rest_5_) | copy-start | bytes 24580
  3.9 1.1 %copy-start.3 = (bf16[4096,128]{1,0:T(8,128)(2,1)}, bf16[4096,128]{1,0:T(8,128)(2,1)S(1)}, u32[]{:S(2)}) copy-start(bf16[4096,128]{1,0:T(8,128)(2,1)S(1)} %collective-permute-done.rest_2_) | copy-start | bytes 3145732
  4.6 20.2 %collective-permute-start.3 = (bf16[4096,512]{1,0:T(8,128)(2,1)}, bf16[4096,512]{1,0:T(8,128)(2,1)}, u32[]{:S(2)}, u32[]{:S(2)}) collective-permute-start(bf16[4096,512]{1,0:T(8,128)(2,1)} %weights_hbm.1), channel_id=1, source_target_pairs={{0,1},{1,0},{2,3},{3,2},{4,5},{5,4},{6,7},{7,6},{8,9},{9,8},{10,11... | collective-permute-start | bytes 12582920 | tf_op jit(solution)/shard_map/ppermute | solution.py:505
  11.9 12.3 %collective-permute-start.8 = (bf16[272,256]{1,0:T(8,128)(2,1)}, bf16[272,256]{1,0:T(8,128)(2,1)S(1)}, u32[]{:S(2)}, u32[]{:S(2)}) collective-permute-start(bf16[272,256]{1,0:T(8,128)(2,1)} %get-tuple-element.16.rest_3_), channel_id=1, source_target_pairs={{0,12},{2,14},{4,0},{6,2},{8,4},{10,6},{12,8},{14,10},{1,13},{3,15... | collective-permute-start | bytes 417800 | tf_op jit(solution)/shard_map/ppermute | solution.py:510
  17.5 12.5 %collective-permute-start.4 = (bf16[272,256]{1,0:T(8,128)(2,1)}, bf16[272,256]{1,0:T(8,128)(2,1)S(1)}, u32[]{:S(2)}, u32[]{:S(2)}) collective-permute-start(bf16[272,256]{1,0:T(8,128)(2,1)} %get-tuple-element.16.rest_3_), channel_id=1, source_target_pairs={{0,8},{2,10},{4,12},{6,14},{8,0},{10,2},{12,4},{14,6},{1,9},{3,11}... | collective-permute-start | bytes 417800 | tf_op jit(solution)/shard_map/ppermute | solution.py:510
  17.5 14.1 %collective-permute-start.15 = (bf16[272,256]{1,0:T(8,128)(2,1)}, bf16[272,256]{1,0:T(8,128)(2,1)S(1)}, u32[]{:S(2)}, u32[]{:S(2)}) collective-permute-start(bf16[272,256]{1,0:T(8,128)(2,1)} %get-tuple-element.16.rest_3_), channel_id=1, source_target_pairs={{0,4},{2,6},{4,8},{6,10},{8,12},{10,14},{12,0},{14,2},{1,5},{3,7},... | collective-permute-start | bytes 417800 | tf_op jit(solution)/shard_map/ppermute | solution.py:510
  18.5 13.7 %collective-permute-start.13 = (bf16[272,256]{1,0:T(8,128)(2,1)}, bf16[272,256]{1,0:T(8,128)(2,1)S(1)}, u32[]{:S(2)}, u32[]{:S(2)}) collective-permute-start(bf16[272,256]{1,0:T(8,128)(2,1)} %get-tuple-element.16.rest_3_), channel_id=1, source_target_pairs={{0,2},{2,0},{4,6},{6,4},{8,10},{10,8},{12,14},{14,12},{1,3},{3,1},... | collective-permute-start | bytes 417800 | tf_op jit(solution)/shard_map/ppermute | solution.py:515
  24.2 11.0 %copy-start.2 = (bf16[272,256]{1,0:T(8,128)(2,1)S(1)}, bf16[272,256]{1,0:T(8,128)(2,1)}, u32[]{:S(2)}) copy-start(bf16[272,256]{1,0:T(8,128)(2,1)} %get-tuple-element.16.rest_3_) | copy-start | bytes 417796
  24.2 12.2 %copy-start = (bf16[512,256]{1,0:T(8,128)(2,1)S(1)}, bf16[512,256]{1,0:T(8,128)(2,1)}, u32[]{:S(2)}) copy-start(bf16[512,256]{1,0:T(8,128)(2,1)} %constant.109.clone.table) | copy-start | bytes 786436
  24.3 7.8 %collective-permute-start.10 = (bf16[272,256]{1,0:T(8,128)(2,1)S(1)}, bf16[272,256]{1,0:T(8,128)(2,1)S(1)}, u32[]{:S(2)}, u32[]{:S(2)}) collective-permute-start(bf16[272,256]{1,0:T(8,128)(2,1)S(1)} %collective-permute-done.8.rest_4_), channel_id=1, source_target_pairs={{0,2},{2,0},{4,6},{6,4},{8,10},{10,8},{12,14},{14,12},{1,3},{3,1},... | collective-permute-start | bytes 417800 | tf_op jit(solution)/shard_map/ppermute | solution.py:515
  30.0 5.1 %collective-permute-start.6 = (bf16[272,256]{1,0:T(8,128)(2,1)S(1)}, bf16[272,256]{1,0:T(8,128)(2,1)S(1)}, u32[]{:S(2)}, u32[]{:S(2)}) collective-permute-start(bf16[272,256]{1,0:T(8,128)(2,1)S(1)} %collective-permute-done.4.rest_0_), channel_id=1, source_target_pairs={{0,2},{2,0},{4,6},{6,4},{8,10},{10,8},{12,14},{14,12},{1,3},{3,1},... | collective-permute-start | bytes 417800 | tf_op jit(solution)/shard_map/ppermute | solution.py:515
  31.5 3.7 %collective-permute-start.5 = (bf16[272,256]{1,0:T(8,128)(2,1)S(1)}, bf16[272,256]{1,0:T(8,128)(2,1)S(1)}, u32[]{:S(2)}, u32[]{:S(2)}) collective-permute-start(bf16[272,256]{1,0:T(8,128)(2,1)S(1)} %collective-permute-done.4.rest_0_), channel_id=1, source_target_pairs={{0,1},{1,0},{2,3},{3,2},{4,5},{5,4},{6,7},{7,6},{8,9},{9,8},{10,11... | collective-permute-start | bytes 417800 | tf_op jit(solution)/shard_map/ppermute | solution.py:505
  31.6 4.2 %collective-permute-start.9 = (bf16[272,256]{1,0:T(8,128)(2,1)S(1)}, bf16[272,256]{1,0:T(8,128)(2,1)S(1)}, u32[]{:S(2)}, u32[]{:S(2)}) collective-permute-start(bf16[272,256]{1,0:T(8,128)(2,1)S(1)} %collective-permute-done.8.rest_4_), channel_id=1, source_target_pairs={{0,1},{1,0},{2,3},{3,2},{4,5},{5,4},{6,7},{7,6},{8,9},{9,8},{10,11... | collective-permute-start | bytes 417800 | tf_op jit(solution)/shard_map/ppermute | solution.py:505
  32.1 3.8 %collective-permute-start.11 = (bf16[272,256]{1,0:T(8,128)(2,1)S(1)}, bf16[272,256]{1,0:T(8,128)(2,1)S(1)}, u32[]{:S(2)}, u32[]{:S(2)}) collective-permute-start(bf16[272,256]{1,0:T(8,128)(2,1)S(1)} %collective-permute-done.10.rest_6_), channel_id=1, source_target_pairs={{0,1},{1,0},{2,3},{3,2},{4,5},{5,4},{6,7},{7,6},{8,9},{9,8},{10,11... | collective-permute-start | bytes 417800 | tf_op jit(solution)/shard_map/ppermute | solution.py:505
  32.2 9.5 %collective-permute-start.17 = (bf16[272,256]{1,0:T(8,128)(2,1)S(1)}, bf16[272,256]{1,0:T(8,128)(2,1)S(1)}, u32[]{:S(2)}, u32[]{:S(2)}) collective-permute-start(bf16[272,256]{1,0:T(8,128)(2,1)S(1)} %collective-permute-done.15.rest_7_), channel_id=1, source_target_pairs={{0,2},{2,0},{4,6},{6,4},{8,10},{10,8},{12,14},{14,12},{1,3},{3,1},... | collective-permute-start | bytes 417800 | tf_op jit(solution)/shard_map/ppermute | solution.py:515
  35.1 1.4 %collective-permute-start.7 = (bf16[272,256]{1,0:T(8,128)(2,1)S(1)}, bf16[272,256]{1,0:T(8,128)(2,1)S(1)}, u32[]{:S(2)}, u32[]{:S(2)}) collective-permute-start(bf16[272,256]{1,0:T(8,128)(2,1)S(1)} %collective-permute-done.6.rest_2_), channel_id=1, source_target_pairs={{0,1},{1,0},{2,3},{3,2},{4,5},{5,4},{6,7},{7,6},{8,9},{9,8},{10,11... | collective-permute-start | bytes 417800 | tf_op jit(solution)/shard_map/ppermute | solution.py:505
  35.2 6.7 %collective-permute-start.12 = (bf16[272,256]{1,0:T(8,128)(2,1)S(1)}, bf16[272,256]{1,0:T(8,128)(2,1)S(1)}, u32[]{:S(2)}, u32[]{:S(2)}) collective-permute-start(bf16[272,256]{1,0:T(8,128)(2,1)S(1)} %copy-done.2), channel_id=1, source_target_pairs={{0,1},{1,0},{2,3},{3,2},{4,5},{5,4},{6,7},{7,6},{8,9},{9,8},{10,11... | collective-permute-start | bytes 417800 | tf_op jit(solution)/shard_map/ppermute | solution.py:505
  35.8 6.1 %collective-permute-start.16 = (bf16[272,256]{1,0:T(8,128)(2,1)S(1)}, bf16[272,256]{1,0:T(8,128)(2,1)S(1)}, u32[]{:S(2)}, u32[]{:S(2)}) collective-permute-start(bf16[272,256]{1,0:T(8,128)(2,1)S(1)} %collective-permute-done.15.rest_7_), channel_id=1, source_target_pairs={{0,1},{1,0},{2,3},{3,2},{4,5},{5,4},{6,7},{7,6},{8,9},{9,8},{10,11... | collective-permute-start | bytes 417800 | tf_op jit(solution)/shard_map/ppermute | solution.py:505
  35.9 6.1 %collective-permute-start.14 = (bf16[272,256]{1,0:T(8,128)(2,1)S(1)}, bf16[272,256]{1,0:T(8,128)(2,1)S(1)}, u32[]{:S(2)}, u32[]{:S(2)}) collective-permute-start(bf16[272,256]{1,0:T(8,128)(2,1)S(1)} %collective-permute-done.13.rest_5_), channel_id=1, source_target_pairs={{0,1},{1,0},{2,3},{3,2},{4,5},{5,4},{6,7},{7,6},{8,9},{9,8},{10,11... | collective-permute-start | bytes 417800 | tf_op jit(solution)/shard_map/ppermute | solution.py:505
  41.7 1.4 %collective-permute-start.18 = (bf16[272,256]{1,0:T(8,128)(2,1)S(1)}, bf16[272,256]{1,0:T(8,128)(2,1)S(1)}, u32[]{:S(2)}, u32[]{:S(2)}) collective-permute-start(bf16[272,256]{1,0:T(8,128)(2,1)S(1)} %collective-permute-done.17.rest_9_), channel_id=1, source_target_pairs={{0,1},{1,0},{2,3},{3,2},{4,5},{5,4},{6,7},{7,6},{8,9},{9,8},{10,11... | collective-permute-start | bytes 417800 | tf_op jit(solution)/shard_map/ppermute | solution.py:505
  43.1 1.0 %copy-start.1 = (bf16[256,512]{1,0:T(8,128)(2,1)S(1)}, bf16[256,512]{1,0:T(8,128)(2,1)}, u32[]{:S(2)}) copy-start(bf16[256,512]{1,0:T(8,128)(2,1)} %queries_other.1.q_hbm) | copy-start | bytes 786436
where the time goes:
time: 53.4 us; the launch traced here: 53.2 us
  Pallas kernels  29.4 us (55%)
  starting transfers between devices  14 us (26%)
  waiting for transfers between devices  8.49 us (16%)
  local copies, waits for them, and re-layouts  0.97 us (2%)
    pallas_call x1, Pallas kernels, attend(): pl.pallas_call(functools.partial(attention_kernel, count, capacity, seq_c...  8.97 us
    pallas_call x2, Pallas kernels, query_half(): pl.pallas_call(functools.partial(query_kernel, mine), in_specs=[pl.BlockS...  8.29 us
    pallas_call x1, Pallas kernels, keys_and_values(): pl.pallas_call(key_value_kernel, in_specs=[pl.BlockSpec(memory_space=pltp...  6.94 us
    ppermute x3, starting transfers between devices, far(): lax.ppermute(array, 'dp', [(i, (i + shift * 2) % count) for i in range(co...  6.58 us
    pallas_call x1, Pallas kernels, spread_early(): pl.pallas_call(functools.partial(early_kernel, len(pieces), capacity, seq...  5.21 us
    ppermute x12, waiting for transfers between devices, swap_cores(): return lax.ppermute(array, 'fsdp', [(0, 1), (1, 0)])  5.03 us
    ppermute x4, starting transfers between devices, swap_near(): return lax.ppermute(array, 'dp', [(i, i ^ 1) for i in range(count)])  4.12 us
    ppermute x12, starting transfers between devices, swap_cores(): return lax.ppermute(array, 'fsdp', [(0, 1), (1, 0)])  3.27 us
  transfers between devices with their start and end apart: 19, of which 6 were waited for; matrix products, arithmetic and copies ran while one was open for 0% of the time, Pallas kernels for 38%

commit v1 on v0

--- a/solution.py
+++ b/solution.py
@@ -46,11 +46,37 @@
     return np.concatenate(terms, axis=1)
 
 
+def facts_kernel(host_ref, slot_ref, out_ref):
+    host = host_ref[...][None, :]
+    rows = host.shape[1]
+    at_row = lax.broadcasted_iota(i32, (rows, rows), 0)
+    at_lane = lax.broadcasted_iota(i32, (rows, rows), 1)
+    column = jnp.sum(jnp.where(at_row == at_lane, host, 0), axis=1, keepdims=True)
+    before = at_row < at_lane
+    same_host = (column == host) & before
+    rank = jnp.sum(jnp.where(same_host, 1, 0), axis=0, keepdims=True)
+    line = lax.broadcasted_iota(i32, out_ref.shape, 0)
+    facts = jnp.where(line == 0, host, jnp.where(line == 1, slot_ref[...][None, :], 0))
+    facts = jnp.where(line == 2, rank, facts)
+    out_ref[...] = facts.astype(f32).astype(bf16)
+
+
+def facts_of(row_host, row_slot):
+    vmem = pl.BlockSpec(memory_space=pltpu.VMEM)
+    return pl.pallas_call(
+        facts_kernel,
+        in_specs=[vmem, vmem],
+        out_shape=jax.ShapeDtypeStruct((FACTS, row_host.shape[0]), bf16),
+        compiler_params=params(8),
+        name="facts",
+    )(row_host, row_slot)
+
+
 def key_value_kernel(core_ref, hidden_hbm, *rest):
-    weights_hbm, small_hbm, rest = rest[:4], rest[4:10], rest[10:]
+    weights_hbm, small_hbm, rest = rest[:4], rest[4:9], rest[9:]
     out_ref, normed_hbm, hidden, normed, gains, wk, wv, wk_other, wv_other, *rest = rest
-    small, (in_sems, sems, out_sems) = rest[:6], rest[6:]
-    gain_ref, gain_other_ref, bk_ref, bv_ref, host_ref, slot_ref = small
+    small, (in_sems, sems, out_sems) = rest[:5], rest[5:]
+    gain_ref, gain_other_ref, bk_ref, bv_ref, facts_ref = small
     rows, width = hidden.shape
     half = width // 2
     core = core_ref[0]
@@ -76,10 +102,7 @@
         c.wait()
     gains[:, pl.ds(own_at, half)] = jnp.broadcast_to(gain_ref[...].astype(f32)[None, :], (high, half))
     gains[:, pl.ds(other_at, half)] = jnp.broadcast_to(gain_other_ref[...].astype(f32)[None, :], (high, half))
-    tail = out_ref.shape[0] - rows
-    line = lax.broadcasted_iota(i32, (tail, rows), 0)
-    facts = jnp.where(line == 0, host_ref[...][None, :], jnp.where(line == 1, slot_ref[...][None, :], 0))
-    out_ref[rows:, :] = facts.astype(f32).astype(bf16)
+    out_ref[rows:, :] = facts_ref[...]
 
     for i in range(parts):
         at = slice(i * part_rows, (i + 1) * part_rows)
@@ -201,31 +224,28 @@
     def __init__(self, pieces, rows, capacity, seq_count, lower_ref, usable_ref, before_count, first):
         self.pieces = pieces
         count = len(pieces)
-        shift = SLOTS_PER_HOST.bit_length() - 1
         facts = [p[rows:, :].astype(f32) for p in pieces]
         hosts = jnp.concatenate([f[0:1] for f in facts], axis=0).astype(i32)
         seqs = hosts * SLOTS_PER_HOST + jnp.concatenate([f[1:2] for f in facts], axis=0).astype(i32)
+        host_ranks = jnp.concatenate([f[2:3] for f in facts], axis=0).astype(i32)
         padded = jnp.concatenate([seqs, jnp.zeros((HD - count, rows), i32)], axis=0)
         columns = jnp.transpose(padded.astype(f32)).astype(i32)
         at_row = lax.broadcasted_iota(i32, (rows, rows), 0)
         at_lane = lax.broadcasted_iota(i32, (rows, rows), 1)
-        before = jnp.where(at_row < at_lane, 1, 0)
         below = jnp.where(at_lane < at_row, 1.0, 0.0).astype(bf16)
         seq_lanes = lax.broadcasted_iota(i32, (rows, seq_count), 1)
         code_lanes = lax.broadcasted_iota(i32, (rows, HD), 1)
         codes_in_block = SLOTS_PER_HOST * BLOCK // capacity
         hots, counts, self.slots, self.marks = [], [], [], []
         for p in range(count):
-            column = columns[:, p : p + 1]
+            column = jnp.broadcast_to(columns[:, p : p + 1], (rows, HD))
             hot = jnp.where(seq_lanes == column, 1.0, 0.0)
             hots.append(hot)
             counts.append(jnp.sum(hot, axis=0, keepdims=True))
-            same = lax.shift_right_logical(column, shift) == hosts[p : p + 1, :]
-            rank = jnp.sum(jnp.where(same, before, 0), axis=0, keepdims=True)
-            self.slots.append(hosts[p : p + 1, :] * capacity + rank)
-            code = jnp.where(usable_ref[first + p] > 0, lax.bitwise_and(column, codes_in_block - 1), -1)
-            mark = (code_lanes == code) | ((code_lanes == HD - 1) & (code >= 0))
-            self.marks.append(jnp.where(mark, 1.0, 0.0).astype(bf16))
+            self.slots.append(hosts[p : p + 1, :] * capacity + host_ranks[p : p + 1, :])
+            mark = (code_lanes == lax.bitwise_and(column, codes_in_block - 1)) | (code_lanes == HD - 1)
+            here = jnp.where(usable_ref[first + p] > 0, 1.0, 0.0)
+            self.marks.append(jnp.where(mark, here, 0.0).astype(bf16))
         base = jnp.zeros((count, seq_count), f32) + before_count
         for q in range(count):
             base = base + lower_ref[first : first + count, first + q : first + q + 1] * counts[q]
@@ -540,11 +560,12 @@
     gain_other = swap_cores(norm_gain)
     w_value_other = swap_cores(w_value)
     w_key_other = swap_cores(w_key)
+    facts = facts_of(row_host, row_slot)
     pairs, normed = keys_and_values(
         which, hidden, w_key, w_value, w_key_other, w_value_other,
-        norm_gain, gain_other, b_key, b_value, row_host, row_slot,
-    )
-    w_query_other = swap_cores(after(w_query, w_key_other, w_value_other, gain_other))
+        norm_gain, gain_other, b_key, b_value, facts,
+    )
+    w_query_other = swap_cores(after(w_query, w_key_other, w_value_other, gain_other, facts))
     first_half = query_half(True, which, normed, w_query)
     lines = {0: pairs}
     for shift in (2, 3, 1):

time: 53.4 us -> 52.3 us (0.979)
  waiting for transfers between devices: 8.49 us -> 6.39 us
  local copies, waits for them, and re-layouts: 0.97 us -> 2.92 us
  Pallas kernels: 29.4 us -> 28.4 us
    ppermute x12, waiting for transfers between devices: 5.03 us -> 2.91 us  [swap_cores(): return lax.ppermute(array, 'fsdp', [(0, 1), (1, 0)])]
    unnamed x10 -> x16, local copies, waits for them, and re-layouts: 0.97 us -> 2.92 us
    pallas_call x1, Pallas kernels: 5.21 us -> 4.64 us  [spread_early(): pl.pallas_call(functools.partial(early_kernel, len(pieces), capacity, seq...]
where the time goes in v1:
time: 52.3 us; the launch traced here: 52.1 us
  Pallas kernels  28.4 us (54%)
  starting transfers between devices  13.9 us (27%)
  waiting for transfers between devices  6.39 us (12%)
  local copies, waits for them, and re-layouts  2.92 us (6%)
    pallas_call x1, Pallas kernels, attend(): pl.pallas_call(functools.partial(attention_kernel, count, capacity, seq_c...  8.44 us
    pallas_call x2, Pallas kernels, query_half(): pl.pallas_call(functools.partial(query_kernel, mine), in_specs=[pl.BlockS...  8.3 us
    pallas_call x1, Pallas kernels, keys_and_values(): pl.pallas_call(key_value_kernel, in_specs=[pl.BlockSpec(memory_space=pltp...  6.91 us
    ppermute x3, starting transfers between devices, far(): lax.ppermute(array, 'dp', [(i, (i + shift * 2) % count) for i in range(co...  6.55 us
    pallas_call x1, Pallas kernels, spread_early(): pl.pallas_call(functools.partial(early_kernel, len(pieces), capacity, seq...  4.64 us
    ppermute x4, starting transfers between devices, swap_near(): return lax.ppermute(array, 'dp', [(i, i ^ 1) for i in range(count)])  4.12 us
    ppermute x12, starting transfers between devices, swap_cores(): return lax.ppermute(array, 'fsdp', [(0, 1), (1, 0)])  3.28 us
    unnamed x16, local copies, waits for them, and re-layouts  2.92 us
  transfers between devices with their start and end apart: 19, of which 6 were waited for; matrix products, arithmetic and copies ran while one was open for 0% of the time, Pallas kernels for 38%

profile of v1, /device:TPU:0, one launch (start us, length us, event | category | flops | bytes accessed | tf_op | source)
XLA Modules:
  0.0 52.1 jit_solution(15333244944598655816)
XLA Ops:
  0.0 0.5 collective-permute-start
  0.5 0.5 collective-permute-start.2
  1.0 0.7 %copy-done.4 = s32[256]{0:T(256)S(1)} copy-done((s32[256]{0:T(256)S(1)}, s32[256]{0:T(256)}, u32[]{:S(2)}) %copy-start.4) | copy-done | bytes 1048
  1.6 0.7 %copy-done.5 = s32[256]{0:T(256)S(1)} copy-done((s32[256]{0:T(256)S(1)}, s32[256]{0:T(256)}, u32[]{:S(2)}) %copy-start.5) | copy-done | bytes 1048
  2.3 0.2 facts.1.rest_8_
  2.5 0.6 %copy-done.3 = bf16[16,256]{1,0:T(8,128)(2,1)} copy-done((bf16[16,256]{1,0:T(8,128)(2,1)}, bf16[16,256]{1,0:T(8,128)(2,1)S(1)}, u32[]{:S(2)}) %copy-start.3) | copy-done | bytes 8216
  3.1 0.8 %collective-permute-done.2.rest_5_ = bf16[4096]{0:T(1024)(128)(2,1)S(1)} collective-permute-done((bf16[4096]{0:T(1024)(128)(2,1)}, bf16[4096]{0:T(1024)(128)(2,1)S(1)}, u32[]{:S(2)}, u32[]{:S(2)}) %collective-permute-start.2) | collective-permute-done | bytes 8224 | tf_op jit(solution)/shard_map/ppermute | solution.py:525
  3.9 0.7 %collective-permute-done.1.rest_3_ = bf16[4096,128]{1,0:T(8,128)(2,1)} collective-permute-done((bf16[4096,128]{1,0:T(8,128)(2,1)}, bf16[4096,128]{1,0:T(8,128)(2,1)}, u32[]{:S(2)}, u32[]{:S(2)}) %collective-permute-start.1) | collective-permute-done | bytes 1048608 | tf_op jit(solution)/shard_map/ppermute | solution.py:525
  4.6 0.4 collective-permute-start.3
  5.0 6.9 %keys_values.1 = (bf16[272,256]{1,0:T(8,128)(2,1)}, bf16[256,8192]{1,0:T(8,128)(2,1)}) custom-call(s32[1]{0:T(128)} %bitcast.core_ref, bf16[256,8192]{1,0:T(8,128)(2,1)} %hidden_hbm.1, bf16[4096,128]{1,0:T(8,128)(2,1)} %rest_0_.1, bf16[4096,128]{1,0:T(8,128)(2,1)} %rest_1_.2, bf16[4096,128]{1,0:T(8,128)(2,1)} %copy-done.6, ...), custom_call_target="tpu_custom_call" | custom-call | flops 1073741824 | bytes 10485760 | tf_op jit(solution)/shard_map/keys_values/pallas_call | solution.py:144
  11.9 5.5 %collective-permute-start.8 = (bf16[272,256]{1,0:T(8,128)(2,1)}, bf16[272,256]{1,0:T(8,128)(2,1)S(1)}, u32[]{:S(2)}, u32[]{:S(2)}) collective-permute-start(bf16[272,256]{1,0:T(8,128)(2,1)} %get-tuple-element.16.rest_3_), channel_id=1, source_target_pairs={{0,12},{2,14},{4,0},{6,2},{8,4},{10,6},{12,8},{14,10},{1,13},{3,15... | collective-permute-start | bytes 417800 | tf_op jit(solution)/shard_map/ppermute | solution.py:530
  17.4 1.0 %collective-permute-start.15 = (bf16[272,256]{1,0:T(8,128)(2,1)}, bf16[272,256]{1,0:T(8,128)(2,1)S(1)}, u32[]{:S(2)}, u32[]{:S(2)}) collective-permute-start(bf16[272,256]{1,0:T(8,128)(2,1)} %get-tuple-element.16.rest_3_), channel_id=1, source_target_pairs={{0,4},{2,6},{4,8},{6,10},{8,12},{10,14},{12,0},{14,2},{1,5},{3,7},... | collective-permute-start | bytes 417800 | tf_op jit(solution)/shard_map/ppermute | solution.py:530
  18.4 1.5 %collective-permute-start.13 = (bf16[272,256]{1,0:T(8,128)(2,1)}, bf16[272,256]{1,0:T(8,128)(2,1)S(1)}, u32[]{:S(2)}, u32[]{:S(2)}) collective-permute-start(bf16[272,256]{1,0:T(8,128)(2,1)} %get-tuple-element.16.rest_3_), channel_id=1, source_target_pairs={{0,2},{2,0},{4,6},{6,4},{8,10},{10,8},{12,14},{14,12},{1,3},{3,1},... | collective-permute-start | bytes 417800 | tf_op jit(solution)/shard_map/ppermute | solution.py:535
  20.0 4.2 %queries_own.1.rest_0_ = f32[256,512]{1,0:T(8,128)} custom-call(s32[1]{0:T(128)} %bitcast.core_ref, bf16[256,8192]{1,0:T(8,128)(2,1)} %get-tuple-element.14.rows_hbm, bf16[4096,512]{1,0:T(8,128)(2,1)} %weights_hbm.1), custom_call_target="tpu_custom_call" | custom-call | flops 1073741824 | bytes 6291456 | tf_op jit(solution)/shard_map/queries_own/pallas_call | solution.py:207
  24.2 0.6 %collective-permute-start.10 = (bf16[272,256]{1,0:T(8,128)(2,1)S(1)}, bf16[272,256]{1,0:T(8,128)(2,1)S(1)}, u32[]{:S(2)}, u32[]{:S(2)}) collective-permute-start(bf16[272,256]{1,0:T(8,128)(2,1)S(1)} %collective-permute-done.8.rest_4_), channel_id=1, source_target_pairs={{0,2},{2,0},{4,6},{6,4},{8,10},{10,8},{12,14},{14,12},{1,3},{3,1},... | collective-permute-start | bytes 417800 | tf_op jit(solution)/shard_map/ppermute | solution.py:535
  24.8 4.1 %queries_other.1.q_hbm = bf16[256,512]{1,0:T(8,128)(2,1)} custom-call(s32[1]{0:T(128)} %bitcast.core_ref, bf16[256,8192]{1,0:T(8,128)(2,1)} %get-tuple-element.14.rows_hbm, bf16[4096,512]{1,0:T(8,128)(2,1)} %collective-permute-done.3.weights_hbm, f32[256,512]{1,0:T(8,128)} %queries_own.1.rest_0_, bf16[512]{0:T(512)(128)(2,1)} %rest_1_.3), custom_call_target="tpu_custom_call" | custom-call | flops 1073741824 | bytes 6291456 | tf_op jit(solution)/shard_map/queries_other/pallas_call | solution.py:207
  28.9 1.1 %collective-permute-done.4.rest_0_ = bf16[272,256]{1,0:T(8,128)(2,1)S(1)} collective-permute-done((bf16[272,256]{1,0:T(8,128)(2,1)}, bf16[272,256]{1,0:T(8,128)(2,1)S(1)}, u32[]{:S(2)}, u32[]{:S(2)}) %collective-permute-start.4) | collective-permute-done | bytes 139296 | tf_op jit(solution)/shard_map/ppermute | solution.py:530
  29.9 1.5 %collective-permute-start.6 = (bf16[272,256]{1,0:T(8,128)(2,1)S(1)}, bf16[272,256]{1,0:T(8,128)(2,1)S(1)}, u32[]{:S(2)}, u32[]{:S(2)}) collective-permute-start(bf16[272,256]{1,0:T(8,128)(2,1)S(1)} %collective-permute-done.4.rest_0_), channel_id=1, source_target_pairs={{0,2},{2,0},{4,6},{6,4},{8,10},{10,8},{12,14},{14,12},{1,3},{3,1},... | collective-permute-start | bytes 417800 | tf_op jit(solution)/shard_map/ppermute | solution.py:535
  31.6 0.5 collective-permute-start.9
  32.1 0.1 collective-permute-start.11
  32.1 0.5 collective-permute-start.17
  32.7 2.4 %collective-permute-done.6.rest_2_ = bf16[272,256]{1,0:T(8,128)(2,1)S(1)} collective-permute-done((bf16[272,256]{1,0:T(8,128)(2,1)S(1)}, bf16[272,256]{1,0:T(8,128)(2,1)S(1)}, u32[]{:S(2)}, u32[]{:S(2)}) %collective-permute-start.6) | collective-permute-done | bytes 139296 | tf_op jit(solution)/shard_map/ppermute | solution.py:535
  35.1 0.1 and_convert_fusion.lower_ref
  35.2 0.6 %collective-permute-start.12 = (bf16[272,256]{1,0:T(8,128)(2,1)S(1)}, bf16[272,256]{1,0:T(8,128)(2,1)S(1)}, u32[]{:S(2)}, u32[]{:S(2)}) collective-permute-start(bf16[272,256]{1,0:T(8,128)(2,1)S(1)} %copy-done.2), channel_id=1, source_target_pairs={{0,1},{1,0},{2,3},{3,2},{4,5},{5,4},{6,7},{7,6},{8,9},{9,8},{10,11... | collective-permute-start | bytes 417800 | tf_op jit(solution)/shard_map/ppermute | solution.py:525
  35.7 0.1 collective-permute-start.16
  35.8 0.4 collective-permute-start.14
  36.2 0.2 collective-permute-done.7.rest_3_
  36.4 4.6 %spread_early.1 = (bf16[16,256,256]{2,1,0:T(8,128)(2,1)S(1)}, bf16[16,256,128]{2,1,0:T(8,128)(2,1)S(1)}, f32[1,128]{1,0:T(1,128)S(1)}) custom-call(s32[16]{0:T(128)S(1)} %get-tuple-element.24.usable_ref, bf16[512,256]{1,0:T(8,128)(2,1)S(1)} %copy-done, f32[16,16]{1,0:T(8,128)S(1)} %and_convert_fusion.lower_ref, ...), custom_call_target="tpu_custom_call" | custom-call | tf_op jit(solution)/shard_map/spread_early/pallas_call | solution.py:317
  41.1 0.2 collective-permute-start.18
  41.3 1.2 %collective-permute-done.18.rest_10_ = bf16[272,256]{1,0:T(8,128)(2,1)S(1)} collective-permute-done((bf16[272,256]{1,0:T(8,128)(2,1)S(1)}, bf16[272,256]{1,0:T(8,128)(2,1)S(1)}, u32[]{:S(2)}, u32[]{:S(2)}) %collective-permute-start.18) | collective-permute-done | bytes 139296 | tf_op jit(solution)/shard_map/ppermute | solution.py:525
  42.5 0.9 %copy-done.1 = bf16[256,512]{1,0:T(8,128)(2,1)S(1)} copy-done((bf16[256,512]{1,0:T(8,128)(2,1)S(1)}, bf16[256,512]{1,0:T(8,128)(2,1)}, u32[]{:S(2)}) %copy-start.1) | copy-done | bytes 262168
  43.5 8.4 %attention.1 = bf16[256,512]{1,0:T(8,128)(2,1)} custom-call(s32[16]{0:T(128)S(1)} %get-tuple-element.24.usable_ref, bf16[512,256]{1,0:T(8,128)(2,1)S(1)} %copy-done, f32[16,16]{1,0:T(8,128)S(1)} %and_convert_fusion.lower_ref, bf16[256,512]{1,0:T(8,128)(2,1)S(1)} %copy-done.1, bf16[16,256,256]{2,1,0:T(8,128)(2,1)S(1)} %get-tuple-element.18.rest_0_, ...), custom_call_target="tpu_custom_call" | custom-call | tf_op jit(solution)/shard_map/attention/pallas_call | solution.py:393
  (30 shorter events, 0.2 us)
Async XLA Ops:
  0.0 3.9 %collective-permute-start = (bf16[4096,128]{1,0:T(8,128)(2,1)}, bf16[4096,128]{1,0:T(8,128)(2,1)S(1)}, u32[]{:S(2)}, u32[]{:S(2)}) collective-permute-start(bf16[4096,128]{1,0:T(8,128)(2,1)} %rest_0_.1), channel_id=1, source_target_pairs={{0,1},{1,0},{2,3},{3,2},{4,5},{5,4},{6,7},{7,6},{8,9},{9,8},{10,11... | collective-permute-start | bytes 3145736 | tf_op jit(solution)/shard_map/ppermute | solution.py:525
  0.5 4.1 %collective-permute-start.1 = (bf16[4096,128]{1,0:T(8,128)(2,1)}, bf16[4096,128]{1,0:T(8,128)(2,1)}, u32[]{:S(2)}, u32[]{:S(2)}) collective-permute-start(bf16[4096,128]{1,0:T(8,128)(2,1)} %rest_1_.2), channel_id=1, source_target_pairs={{0,1},{1,0},{2,3},{3,2},{4,5},{5,4},{6,7},{7,6},{8,9},{9,8},{10,11... | collective-permute-start | bytes 3145736 | tf_op jit(solution)/shard_map/ppermute | solution.py:525
  0.5 3.4 %collective-permute-start.2 = (bf16[4096]{0:T(1024)(128)(2,1)}, bf16[4096]{0:T(1024)(128)(2,1)S(1)}, u32[]{:S(2)}, u32[]{:S(2)}) collective-permute-start(bf16[4096]{0:T(1024)(128)(2,1)} %rest_4_.1), channel_id=1, source_target_pairs={{0,1},{1,0},{2,3},{3,2},{4,5},{5,4},{6,7},{7,6},{8,9},{9,8},{10,11... | collective-permute-start | bytes 24584 | tf_op jit(solution)/shard_map/ppermute | solution.py:525
  1.0 0.7 %copy-start.4 = (s32[256]{0:T(256)S(1)}, s32[256]{0:T(256)}, u32[]{:S(2)}) copy-start(s32[256]{0:T(256)} %host_ref.1) | copy-start | bytes 3076
  1.6 0.7 %copy-start.5 = (s32[256]{0:T(256)S(1)}, s32[256]{0:T(256)}, u32[]{:S(2)}) copy-start(s32[256]{0:T(256)} %slot_ref.1) | copy-start | bytes 3076
  2.5 0.6 %copy-start.3 = (bf16[16,256]{1,0:T(8,128)(2,1)}, bf16[16,256]{1,0:T(8,128)(2,1)S(1)}, u32[]{:S(2)}) copy-start(bf16[16,256]{1,0:T(8,128)(2,1)S(1)} %facts.1.rest_8_) | copy-start | bytes 24580
  3.9 1.1 %copy-start.7 = (bf16[4096]{0:T(1024)(128)(2,1)}, bf16[4096]{0:T(1024)(128)(2,1)S(1)}, u32[]{:S(2)}) copy-start(bf16[4096]{0:T(1024)(128)(2,1)S(1)} %collective-permute-done.2.rest_5_) | copy-start | bytes 24580
  3.9 1.1 %copy-start.6 = (bf16[4096,128]{1,0:T(8,128)(2,1)}, bf16[4096,128]{1,0:T(8,128)(2,1)S(1)}, u32[]{:S(2)}) copy-start(bf16[4096,128]{1,0:T(8,128)(2,1)S(1)} %collective-permute-done.rest_2_) | copy-start | bytes 3145732
  4.6 20.2 %collective-permute-start.3 = (bf16[4096,512]{1,0:T(8,128)(2,1)}, bf16[4096,512]{1,0:T(8,128)(2,1)}, u32[]{:S(2)}, u32[]{:S(2)}) collective-permute-start(bf16[4096,512]{1,0:T(8,128)(2,1)} %weights_hbm.1), channel_id=1, source_target_pairs={{0,1},{1,0},{2,3},{3,2},{4,5},{5,4},{6,7},{7,6},{8,9},{9,8},{10,11... | collective-permute-start | bytes 12582920 | tf_op jit(solution)/shard_map/ppermute | solution.py:525
  11.9 12.3 %collective-permute-start.8 = (bf16[272,256]{1,0:T(8,128)(2,1)}, bf16[272,256]{1,0:T(8,128)(2,1)S(1)}, u32[]{:S(2)}, u32[]{:S(2)}) collective-permute-start(bf16[272,256]{1,0:T(8,128)(2,1)} %get-tuple-element.16.rest_3_), channel_id=1, source_target_pairs={{0,12},{2,14},{4,0},{6,2},{8,4},{10,6},{12,8},{14,10},{1,13},{3,15... | collective-permute-start | bytes 417800 | tf_op jit(solution)/shard_map/ppermute | solution.py:530
  17.4 12.5 %collective-permute-start.4 = (bf16[272,256]{1,0:T(8,128)(2,1)}, bf16[272,256]{1,0:T(8,128)(2,1)S(1)}, u32[]{:S(2)}, u32[]{:S(2)}) collective-permute-start(bf16[272,256]{1,0:T(8,128)(2,1)} %get-tuple-element.16.rest_3_), channel_id=1, source_target_pairs={{0,8},{2,10},{4,12},{6,14},{8,0},{10,2},{12,4},{14,6},{1,9},{3,11}... | collective-permute-start | bytes 417800 | tf_op jit(solution)/shard_map/ppermute | solution.py:530
  17.4 14.1 %collective-permute-start.15 = (bf16[272,256]{1,0:T(8,128)(2,1)}, bf16[272,256]{1,0:T(8,128)(2,1)S(1)}, u32[]{:S(2)}, u32[]{:S(2)}) collective-permute-start(bf16[272,256]{1,0:T(8,128)(2,1)} %get-tuple-element.16.rest_3_), channel_id=1, source_target_pairs={{0,4},{2,6},{4,8},{6,10},{8,12},{10,14},{12,0},{14,2},{1,5},{3,7},... | collective-permute-start | bytes 417800 | tf_op jit(solution)/shard_map/ppermute | solution.py:530
  18.4 13.7 %collective-permute-start.13 = (bf16[272,256]{1,0:T(8,128)(2,1)}, bf16[272,256]{1,0:T(8,128)(2,1)S(1)}, u32[]{:S(2)}, u32[]{:S(2)}) collective-permute-start(bf16[272,256]{1,0:T(8,128)(2,1)} %get-tuple-element.16.rest_3_), channel_id=1, source_target_pairs={{0,2},{2,0},{4,6},{6,4},{8,10},{10,8},{12,14},{14,12},{1,3},{3,1},... | collective-permute-start | bytes 417800 | tf_op jit(solution)/shard_map/ppermute | solution.py:535
  24.2 11.0 %copy-start.2 = (bf16[272,256]{1,0:T(8,128)(2,1)S(1)}, bf16[272,256]{1,0:T(8,128)(2,1)}, u32[]{:S(2)}) copy-start(bf16[272,256]{1,0:T(8,128)(2,1)} %get-tuple-element.16.rest_3_) | copy-start | bytes 417796
  24.2 12.2 %copy-start = (bf16[512,256]{1,0:T(8,128)(2,1)S(1)}, bf16[512,256]{1,0:T(8,128)(2,1)}, u32[]{:S(2)}) copy-start(bf16[512,256]{1,0:T(8,128)(2,1)} %constant.109.clone.table) | copy-start | bytes 786436
  24.2 7.8 %collective-permute-start.10 = (bf16[272,256]{1,0:T(8,128)(2,1)S(1)}, bf16[272,256]{1,0:T(8,128)(2,1)S(1)}, u32[]{:S(2)}, u32[]{:S(2)}) collective-permute-start(bf16[272,256]{1,0:T(8,128)(2,1)S(1)} %collective-permute-done.8.rest_4_), channel_id=1, source_target_pairs={{0,2},{2,0},{4,6},{6,4},{8,10},{10,8},{12,14},{14,12},{1,3},{3,1},... | collective-permute-start | bytes 417800 | tf_op jit(solution)/shard_map/ppermute | solution.py:535
  29.9 5.1 %collective-permute-start.6 = (bf16[272,256]{1,0:T(8,128)(2,1)S(1)}, bf16[272,256]{1,0:T(8,128)(2,1)S(1)}, u32[]{:S(2)}, u32[]{:S(2)}) collective-permute-start(bf16[272,256]{1,0:T(8,128)(2,1)S(1)} %collective-permute-done.4.rest_0_), channel_id=1, source_target_pairs={{0,2},{2,0},{4,6},{6,4},{8,10},{10,8},{12,14},{14,12},{1,3},{3,1},... | collective-permute-start | bytes 417800 | tf_op jit(solution)/shard_map/ppermute | solution.py:535
  31.5 3.7 %collective-permute-start.5 = (bf16[272,256]{1,0:T(8,128)(2,1)S(1)}, bf16[272,256]{1,0:T(8,128)(2,1)S(1)}, u32[]{:S(2)}, u32[]{:S(2)}) collective-permute-start(bf16[272,256]{1,0:T(8,128)(2,1)S(1)} %collective-permute-done.4.rest_0_), channel_id=1, source_target_pairs={{0,1},{1,0},{2,3},{3,2},{4,5},{5,4},{6,7},{7,6},{8,9},{9,8},{10,11... | collective-permute-start | bytes 417800 | tf_op jit(solution)/shard_map/ppermute | solution.py:525
  31.6 4.2 %collective-permute-start.9 = (bf16[272,256]{1,0:T(8,128)(2,1)S(1)}, bf16[272,256]{1,0:T(8,128)(2,1)S(1)}, u32[]{:S(2)}, u32[]{:S(2)}) collective-permute-start(bf16[272,256]{1,0:T(8,128)(2,1)S(1)} %collective-permute-done.8.rest_4_), channel_id=1, source_target_pairs={{0,1},{1,0},{2,3},{3,2},{4,5},{5,4},{6,7},{7,6},{8,9},{9,8},{10,11... | collective-permute-start | bytes 417800 | tf_op jit(solution)/shard_map/ppermute | solution.py:525
  32.1 3.8 %collective-permute-start.11 = (bf16[272,256]{1,0:T(8,128)(2,1)S(1)}, bf16[272,256]{1,0:T(8,128)(2,1)S(1)}, u32[]{:S(2)}, u32[]{:S(2)}) collective-permute-start(bf16[272,256]{1,0:T(8,128)(2,1)S(1)} %collective-permute-done.10.rest_6_), channel_id=1, source_target_pairs={{0,1},{1,0},{2,3},{3,2},{4,5},{5,4},{6,7},{7,6},{8,9},{9,8},{10,11... | collective-permute-start | bytes 417800 | tf_op jit(solution)/shard_map/ppermute | solution.py:525
  32.1 8.9 %collective-permute-start.17 = (bf16[272,256]{1,0:T(8,128)(2,1)S(1)}, bf16[272,256]{1,0:T(8,128)(2,1)S(1)}, u32[]{:S(2)}, u32[]{:S(2)}) collective-permute-start(bf16[272,256]{1,0:T(8,128)(2,1)S(1)} %collective-permute-done.15.rest_7_), channel_id=1, source_target_pairs={{0,2},{2,0},{4,6},{6,4},{8,10},{10,8},{12,14},{14,12},{1,3},{3,1},... | collective-permute-start | bytes 417800 | tf_op jit(solution)/shard_map/ppermute | solution.py:535
  35.1 1.4 %collective-permute-start.7 = (bf16[272,256]{1,0:T(8,128)(2,1)S(1)}, bf16[272,256]{1,0:T(8,128)(2,1)S(1)}, u32[]{:S(2)}, u32[]{:S(2)}) collective-permute-start(bf16[272,256]{1,0:T(8,128)(2,1)S(1)} %collective-permute-done.6.rest_2_), channel_id=1, source_target_pairs={{0,1},{1,0},{2,3},{3,2},{4,5},{5,4},{6,7},{7,6},{8,9},{9,8},{10,11... | collective-permute-start | bytes 417800 | tf_op jit(solution)/shard_map/ppermute | solution.py:525
  35.2 6.1 %collective-permute-start.12 = (bf16[272,256]{1,0:T(8,128)(2,1)S(1)}, bf16[272,256]{1,0:T(8,128)(2,1)S(1)}, u32[]{:S(2)}, u32[]{:S(2)}) collective-permute-start(bf16[272,256]{1,0:T(8,128)(2,1)S(1)} %copy-done.2), channel_id=1, source_target_pairs={{0,1},{1,0},{2,3},{3,2},{4,5},{5,4},{6,7},{7,6},{8,9},{9,8},{10,11... | collective-permute-start | bytes 417800 | tf_op jit(solution)/shard_map/ppermute | solution.py:525
  35.7 5.6 %collective-permute-start.16 = (bf16[272,256]{1,0:T(8,128)(2,1)S(1)}, bf16[272,256]{1,0:T(8,128)(2,1)S(1)}, u32[]{:S(2)}, u32[]{:S(2)}) collective-permute-start(bf16[272,256]{1,0:T(8,128)(2,1)S(1)} %collective-permute-done.15.rest_7_), channel_id=1, source_target_pairs={{0,1},{1,0},{2,3},{3,2},{4,5},{5,4},{6,7},{7,6},{8,9},{9,8},{10,11... | collective-permute-start | bytes 417800 | tf_op jit(solution)/shard_map/ppermute | solution.py:525
  35.8 5.5 %collective-permute-start.14 = (bf16[272,256]{1,0:T(8,128)(2,1)S(1)}, bf16[272,256]{1,0:T(8,128)(2,1)S(1)}, u32[]{:S(2)}, u32[]{:S(2)}) collective-permute-start(bf16[272,256]{1,0:T(8,128)(2,1)S(1)} %collective-permute-done.13.rest_5_), channel_id=1, source_target_pairs={{0,1},{1,0},{2,3},{3,2},{4,5},{5,4},{6,7},{7,6},{8,9},{9,8},{10,11... | collective-permute-start | bytes 417800 | tf_op jit(solution)/shard_map/ppermute | solution.py:525
  41.1 1.4 %collective-permute-start.18 = (bf16[272,256]{1,0:T(8,128)(2,1)S(1)}, bf16[272,256]{1,0:T(8,128)(2,1)S(1)}, u32[]{:S(2)}, u32[]{:S(2)}) collective-permute-start(bf16[272,256]{1,0:T(8,128)(2,1)S(1)} %collective-permute-done.17.rest_9_), channel_id=1, source_target_pairs={{0,1},{1,0},{2,3},{3,2},{4,5},{5,4},{6,7},{7,6},{8,9},{9,8},{10,11... | collective-permute-start | bytes 417800 | tf_op jit(solution)/shard_map/ppermute | solution.py:525
  42.5 1.0 %copy-start.1 = (bf16[256,512]{1,0:T(8,128)(2,1)S(1)}, bf16[256,512]{1,0:T(8,128)(2,1)}, u32[]{:S(2)}) copy-start(bf16[256,512]{1,0:T(8,128)(2,1)} %queries_other.1.q_hbm) | copy-start | bytes 786436
